TPU v7x, 128 devices: a whole 4x4x4 slice. The times are simulated.
128 devices in a mesh: region: 4 (over z), rays: 32 (over x, y, core).
Axes of the slice: x: 4, y: 4, z: 4, core: 2. Of those that a mesh axis runs over, the one named last changes fastest.
Arguments:
- tile_values: float32 [32768, 128, 128], P(('region', 'rays')), may hold values from -0.1875 to 0.1875
- tile_row: int32 [32768], P(('region', 'rays')), may hold values from 0 to 15
- tile_owner: int32 [32768, 1], P(('region', 'rays')), may hold values from 0 to 127; in each aligned block of 256 rows (0 to 255, 256 to 511, ...) at most 2 rows name the same one
- tile_sub: int32 [32768], P(('region', 'rays')), may hold values from 0 to 31
- tile_count: int32 [128], P(('region', 'rays')), may hold values from 128 to 256, as said below
- residual_times: float32 [4, 262144], P(None, ('region', 'rays')), may hold values from -16 to 16
Outputs:
- slowness_update: float32 [4, 524288], P(None, ('region', 'rays'))
- relative_residual: float32 [4], replicated
Inputs may be any that keep to these rules, and one draw needn't show every extreme that they name: `tile_owner`: among the 256 entries of one device, at most 2 name one owner. `tile_count`: each count is 256 or 128, and some device has all 256.
All inputs are finite; a program needn't handle non-finite values.
Results may differ from a plain program's by a relative error of at most 0.0003.
Values sent between devices are 32-bit elements; how exact they have to be, the bound alone decides.
A program may use at most 64 MiB of HBM per device.

v0:
```python
import jax
import jax.numpy as jnp
from jax import lax
from jax.sharding import PartitionSpec as P

CB = 32
ITERS = 2


EPSILON = 1e-06
PRECISE = lax.Precision.HIGHEST


def per_device(tile_values, tile_row, tile_owner, tile_sub, tile_count, residual_times):
    devices = lax.axis_size(("region", "rays"))
    tile_total = tile_values.shape[0]
    tile_side = tile_values.shape[1]
    slot_count = max(2, tile_total // devices)
    capacity = devices * slot_count
    rhs_count = residual_times.shape[0]
    row_blocks = residual_times.shape[1] // tile_side
    owners = tile_owner[:, 0]
    owner_hot = (owners[:, None] == jnp.arange(devices, dtype=jnp.int32)[None, :]).astype(jnp.int32)
    slot_rank = jnp.sum((jnp.cumsum(owner_hot, axis=0) - 1) * owner_hot, axis=1)
    position = owners * slot_count + slot_rank
    request_ids = jnp.zeros((capacity,), jnp.int32).at[position].set(tile_sub)
    live_mask = (jnp.arange(tile_total, dtype=jnp.int32) < tile_count[0]).astype(jnp.float32)
    row_hot = (jnp.arange(row_blocks, dtype=jnp.int32)[:, None] == tile_row[None, :]).astype(
        jnp.float32
    )

    def adjoint_terms(ray_part):
        spread = (
            jnp.einsum("bt,bnr->tnr", row_hot, ray_part, precision=PRECISE)
            * live_mask[:, None, None]
        )
        contribution = jnp.einsum("trc,tnr->tnc", tile_values, spread, precision=PRECISE)
        return (
            jnp.zeros((capacity,) + contribution.shape[1:], jnp.float32)
            .at[position]
            .set(contribution)
        )

    def owner_sum(cell_hot, piece):
        return jnp.einsum("bp,pnc->bnc", cell_hot, piece, precision=PRECISE)

    def squares(values):
        return jnp.sum(values * values, axis=(0, 2))

    def ray_norm(values):
        return jnp.sqrt(lax.psum(squares(values), ("region", "rays")) + EPSILON)

    def model_norm(values):
        return jnp.sqrt(lax.psum(squares(values), ("region", "rays")) + EPSILON)

    def column(scalar):
        return scalar[None, :, None]

    data_part = residual_times.reshape(rhs_count, row_blocks, tile_side).transpose(1, 0, 2)
    beta_now = ray_norm(data_part)
    ray_vec = data_part / column(beta_now)
    arrived = lax.all_to_all(
        adjoint_terms(ray_vec), ("region", "rays"), split_axis=0, concat_axis=0, tiled=True
    )
    arrived_ids = lax.all_to_all(
        request_ids, ("region", "rays"), split_axis=0, concat_axis=0, tiled=True
    )
    cell_hot = (jnp.arange(CB, dtype=jnp.int32)[:, None] == arrived_ids[None, :]).astype(
        jnp.float32
    )
    pushed, cell_hot = (owner_sum(cell_hot, arrived), cell_hot)
    alpha_now = model_norm(pushed)
    model_vec = pushed / column(alpha_now)
    beta_first = beta_now
    direction = model_vec
    solution = jnp.zeros_like(model_vec)
    phi_bar = beta_now
    rho_bar = alpha_now
    for step_index in range(ITERS):
        final_step = step_index + 1 == ITERS
        reply_rows = jnp.einsum("bp,bnc->pnc", cell_hot, model_vec, precision=PRECISE)
        picked = (
            lax.all_to_all(reply_rows, ("region", "rays"), split_axis=0, concat_axis=0, tiled=True)[
                position
            ]
            * live_mask[:, None, None]
        )
        products = jnp.einsum("trc,tnc->tnr", tile_values, picked, precision=PRECISE)
        result = jnp.einsum("bt,tnr->bnr", row_hot, products, precision=PRECISE)
        image_rays = result - column(alpha_now) * ray_vec
        model_next = model_vec
        if final_step:
            beta_now = ray_norm(image_rays)
            ray_vec = image_rays / column(beta_now)
        else:
            beta_now = ray_norm(image_rays)
            ray_vec = image_rays / column(beta_now)
            push_result = owner_sum(
                cell_hot,
                lax.all_to_all(
                    adjoint_terms(ray_vec),
                    ("region", "rays"),
                    split_axis=0,
                    concat_axis=0,
                    tiled=True,
                ),
            )
            pushed = push_result - column(beta_now) * model_vec
            alpha_now = model_norm(pushed)
            model_next = pushed / column(alpha_now)
        rho_now = jnp.sqrt(rho_bar * rho_bar + beta_now * beta_now)
        cosine = rho_bar / rho_now
        sine_value = beta_now / rho_now
        phi_now = cosine * phi_bar
        phi_bar = sine_value * phi_bar
        solution = solution + column(phi_now / rho_now) * direction
        if not final_step:
            theta_now = sine_value * alpha_now
            rho_bar = -cosine * alpha_now
            direction = model_next - column(theta_now / rho_now) * direction
            model_vec = model_next
    slowness_update = solution.transpose(1, 0, 2).reshape(rhs_count, CB * tile_side)
    return (slowness_update, phi_bar / beta_first)


def solution(mesh):
    placed = (
        P(("region", "rays"), None, None),
        P(("region", "rays")),
        P(("region", "rays"), None),
        P(("region", "rays")),
        P(("region", "rays")),
        P(None, ("region", "rays")),
    )
    return jax.shard_map(
        per_device,
        mesh=mesh,
        in_specs=placed,
        out_specs=(P(None, ("region", "rays")), P()),
        check_vma=False,
    )
```

profile of v0, /device:TPU:1, one launch (start us, length us, event | category | flops | bytes accessed | tf_op | source)
XLA Modules:
  0.0 543.0 jit_solution(17772239960349264786)
XLA Ops:
  3.3 1.6 scatter_custom_fusion
  5.6 11.5 %all-to-all-start = ((s32[128,2,1]{1,2,0:T(1,128)}), s32[128,2,1]{1,2,0:T(1,128)S(1)}, u32[]{:S(2)}, u32[]{:S(2)}) async-start(s32[128,2,1]{1,2,0:T(1,128)} %bitcast.7), calls=%async_computation | async-start | bytes 131072 | tf_op jit(solution)/shard_map/all_to_all | solution.py:65
  17.8 0.9 fusion.19
  18.7 67.2 %psum.35 = f32[4]{0:T(128)S(1)} all-reduce(f32[4]{0:T(128)S(1)} %fusion.19), channel_id=1, replica_groups=mesh['region'=4,'rays'=32] {'region','rays'}, use_global_device_ids=true, to_apply=%region_5.6 | all-reduce | flops 4 | bytes 32 | tf_op jit(solution)/shard_map/psum | solution.py:51
  85.9 1.2 convolution_multiply_fusion.1
  87.1 16.7 %fusion.13 = f32[256,4,128]{2,1,0:T(4,128)S(1)} fusion(f32[256,128,128]{2,1,0:T(8,128)} %param.6, f32[256,4,128]{2,0,1:T(8,128)S(1)} %convolution_multiply_fusion.1), kind=kOutput, calls=%fused_computation.25 | convolution fusion | flops 201326592 | bytes 17825792 | tf_op jit(solution)/shard_map/trc,tnr->tnc/dot_general | solution.py:37
  104.6 24.3 %scatter_fusion = f32[256,4,128]{2,1,0:T(4,128)} fusion(f32[256,4,128]{2,1,0:T(4,128)} %broadcast.68.clone, s32[256]{0:T(256)S(1)} %bitcast.68, f32[256,4,128]{2,1,0:T(4,128)S(1)} %fusion.13), kind=kCustom, calls=%fused_computation.3 | custom fusion | bytes 1573888 | tf_op jit(solution)/shard_map/scatter | solution.py:41
  128.9 4.8 all-to-all-start.1
  135.2 12.0 %all-to-all-done.1 = f32[256,4,128]{2,1,0:T(4,128)S(1)} async-done(((f32[256,4,128]{2,1,0:T(4,128)}), f32[256,4,128]{2,1,0:T(4,128)S(1)}, u32[]{:S(2)}, u32[]{:S(2)}) %all-to-all-start.1) | async-done | bytes 524320 | tf_op jit(solution)/shard_map/all_to_all | solution.py:62
  147.7 63.1 %psum.36 = f32[4]{0:T(128)S(1)} all-reduce(f32[4]{0:T(128)S(1)} %get-tuple-element.9), channel_id=1, replica_groups=mesh['region'=4,'rays'=32] {'region','rays'}, use_global_device_ids=true, to_apply=%region_8.9 | all-reduce | flops 4 | bytes 32 | tf_op jit(solution)/shard_map/psum | solution.py:54
  211.2 1.1 copy.44
  212.3 4.6 all-to-all-start.2
  217.0 13.5 %all-to-all-done.2 = f32[256,4,128]{2,1,0:T(4,128)S(1)} async-done(((f32[256,4,128]{2,1,0:T(4,128)}), f32[256,4,128]{2,1,0:T(4,128)S(1)}, u32[]{:S(2)}, u32[]{:S(2)}) %all-to-all-start.2) | async-done | bytes 524320 | tf_op jit(solution)/shard_map/all_to_all | solution.py:83
  230.5 1.0 gather_fusion
  231.6 28.7 %fusion.9 = f32[256,4,128]{2,1,0:T(4,128)S(1)} fusion(f32[256,128,128]{2,1,0:T(8,128)} %param.6, f32[256,4,128]{2,0,1:T(8,128)S(1)} %copy_multiply_fusion.1), kind=kOutput, calls=%fused_computation.20 | convolution fusion | flops 201326592 | bytes 17825792 | tf_op jit(solution)/shard_map/trc,tnc->tnr/dot_general | solution.py:88
  260.7 63.1 %psum.37 = f32[4]{0:T(128)S(1)} all-reduce(f32[4]{0:T(128)S(1)} %get-tuple-element.11), channel_id=1, replica_groups=mesh['region'=4,'rays'=32] {'region','rays'}, use_global_device_ids=true, to_apply=%region_10.11 | all-reduce | flops 4 | bytes 32 | tf_op jit(solution)/shard_map/psum | solution.py:51
  324.3 16.7 %fusion.6 = f32[256,4,128]{2,1,0:T(4,128)S(1)} fusion(f32[256,128,128]{2,1,0:T(8,128)} %param.6, f32[256,4,128]{2,0,1:T(8,128)S(1)} %convolution_multiply_fusion), kind=kOutput, calls=%fused_computation.17 | convolution fusion | flops 201326592 | bytes 17825792 | tf_op jit(solution)/shard_map/trc,tnr->tnc/dot_general | solution.py:37
  341.0 7.1 %scatter_fusion.1 = f32[256,4,128]{2,1,0:T(4,128)S(1)} fusion(f32[256,4,128]{2,1,0:T(4,128)S(1)} %broadcast.68, s32[256]{0:T(256)S(1)} %bitcast.70, f32[256,4,128]{2,1,0:T(4,128)S(1)} %fusion.6), kind=kCustom, calls=%fused_computation.4 | custom fusion | bytes 1573888 | tf_op jit(solution)/shard_map/scatter | solution.py:41
  348.1 17.9 %all_to_all.29 = f32[256,4,128]{2,1,0:T(4,128)S(1)} all-to-all(f32[256,4,128]{2,1,0:T(4,128)S(1)} %scatter_fusion.1), channel_id=1, replica_groups=mesh['region'=4,'rays'=32] {'region','rays'}, dimensions={0} | all-to-all | bytes 1048576 | tf_op jit(solution)/shard_map/all_to_all | solution.py:100
  366.4 63.1 %psum.38 = f32[4]{0:T(128)S(1)} all-reduce(f32[4]{0:T(128)S(1)} %get-tuple-element.13), channel_id=1, replica_groups=mesh['region'=4,'rays'=32] {'region','rays'}, use_global_device_ids=true, to_apply=%region_13.14 | all-reduce | flops 4 | bytes 32 | tf_op jit(solution)/shard_map/psum | solution.py:54
  430.4 17.9 %all_to_all.30 = f32[256,4,128]{2,1,0:T(4,128)S(1)} all-to-all(f32[256,4,128]{2,1,0:T(4,128)S(1)} %copy.50), channel_id=1, replica_groups=mesh['region'=4,'rays'=32] {'region','rays'}, dimensions={0} | all-to-all | bytes 1048576 | tf_op jit(solution)/shard_map/all_to_all | solution.py:83
  448.3 1.0 gather_fusion.1
  449.4 28.7 %fusion.3 = f32[256,4,128]{2,1,0:T(4,128)S(1)} fusion(f32[256,128,128]{2,1,0:T(8,128)} %param.6, f32[256,4,128]{2,0,1:T(8,128)S(1)} %copy_multiply_fusion), kind=kOutput, calls=%fused_computation.13 | convolution fusion | flops 201326592 | bytes 17825792 | tf_op jit(solution)/shard_map/trc,tnc->tnr/dot_general | solution.py:88
  478.5 63.1 %psum.39 = f32[4]{0:T(128)S(1)} all-reduce(f32[4]{0:T(128)S(1)} %fusion.1), channel_id=1, replica_groups=mesh['region'=4,'rays'=32] {'region','rays'}, use_global_device_ids=true, to_apply=%region_15.16 | all-reduce | flops 4 | bytes 32 | tf_op jit(solution)/shard_map/psum | solution.py:51
  (40 shorter events, 10.8 us)
Async XLA Ops:
  5.6 123.3 %all-to-all-start = ((s32[128,2,1]{1,2,0:T(1,128)}), s32[128,2,1]{1,2,0:T(1,128)S(1)}, u32[]{:S(2)}, u32[]{:S(2)}) async-start(s32[128,2,1]{1,2,0:T(1,128)} %bitcast.7), calls=%async_computation | async-start | bytes 131072 | tf_op jit(solution)/shard_map/all_to_all | solution.py:65
  103.8 156.5 %copy-start = (f32[4,2048]{1,0:T(4,128)S(1)}, f32[4,2048]{1,0:T(4,128)}, u32[]{:S(2)}) copy-start(f32[4,2048]{1,0:T(4,128)} %param.11) | copy-start | bytes 98308
  103.8 156.5 %copy-start.1 = (s32[256]{0:T(256)S(1)}, s32[256]{0:T(256)}, u32[]{:S(2)}) copy-start(s32[256]{0:T(256)} %param.7) | copy-start | bytes 3076
  128.9 18.3 %all-to-all-start.1 = ((f32[256,4,128]{2,1,0:T(4,128)}), f32[256,4,128]{2,1,0:T(4,128)S(1)}, u32[]{:S(2)}, u32[]{:S(2)}) async-start(f32[256,4,128]{2,1,0:T(4,128)} %scatter_fusion), calls=%async_computation.1 | async-start | bytes 1048576 | tf_op jit(solution)/shard_map/all_to_all | solution.py:62
  212.3 18.1 %all-to-all-start.2 = ((f32[256,4,128]{2,1,0:T(4,128)}), f32[256,4,128]{2,1,0:T(4,128)S(1)}, u32[]{:S(2)}, u32[]{:S(2)}) async-start(f32[256,4,128]{2,1,0:T(4,128)} %copy.44), calls=%async_computation.2 | async-start | bytes 1048576 | tf_op jit(solution)/shard_map/all_to_all | solution.py:83
where the time goes:
time: 545 us; the launch traced here: 543 us
  blocking collectives  355 us (65%)
  matrix products  94.9 us (17%)
  local copies, waits for them, and re-layouts  40.2 us (7%)
  waiting for transfers between devices  25.5 us (5%)
  starting transfers between devices  21 us (4%)
    psum x3, blocking collectives, ray_norm(): return jnp.sqrt(lax.psum(squares(values), ('region', 'rays')) + EPSILON)  193 us
    psum x2, blocking collectives, model_norm(): return jnp.sqrt(lax.psum(squares(values), ('region', 'rays')) + EPSILON)  126 us
    dot_general x2, matrix products, per_device(): jnp.einsum('trc,tnc->tnr', tile_values, picked, precision=PRECISE)  57.4 us
    dot_general x2, matrix products, adjoint_terms(): jnp.einsum('trc,tnr->tnc', tile_values, spread, precision=PRECISE)  33.4 us
    scatter x2, local copies, waits for them, and re-layouts, adjoint_terms(): return jnp.zeros((capacity,) + contribution.shape[1:], jnp.float32).at[po...  31.3 us
    all_to_all x1, blocking collectives, per_device(): lax.all_to_all(reply_rows, ('region', 'rays'), split_axis=0, concat_axis=...  17.9 us
    all_to_all x1, blocking collectives, per_device(): lax.all_to_all(adjoint_terms(ray_vec), ('region', 'rays'), split_axis=0,...  17.9 us
    all_to_all x1, waiting for transfers between devices, per_device(): lax.all_to_all(reply_rows, ('region', 'rays'), split_axis=0, concat_axis=...  13.5 us
  transfers between devices with their start and end apart: 3, of which 2 were waited for; matrix products, arithmetic and copies ran while one was open for 8% of the time, Pallas kernels for 0%

commit v1 on v0

v1 whole, which is shorter than its diff:
```python
import functools

import jax
import jax.numpy as jnp
from jax import lax
from jax.experimental import pallas as pl
from jax.experimental.pallas import tpu as pltpu
from jax.sharding import PartitionSpec as P

EPSILON = 1e-06
MESH = pl.DeviceIdType.MESH
F32 = jnp.float32
BF16 = jnp.bfloat16

DEVICES = 128
GROUP = 16
GROUPS = DEVICES // GROUP
STRIDE = 37
UNSTRIDE = pow(STRIDE, -1, DEVICES)
NORMS = 5
LOADS = 8


def my_place():
    z = lax.axis_index("region")
    rays = lax.axis_index("rays")
    return z, rays // 8, (rays // 2) % 4, rays % 2


def partner(k, sign=1):
    z, x, y, c = my_place()
    shift = (k * STRIDE) % DEVICES
    oz = (z + 4 + sign * (shift // 32)) % 4
    ox = (x + 4 + sign * ((shift // 8) % 4)) % 4
    oy = (y + 4 + sign * ((shift // 2) % 4)) % 4
    oc = (c + shift % 2) % 2
    return (oz, ox * 8 + oy * 2 + oc)


def split(values):
    high = values.astype(BF16)
    low = (values - high.astype(F32)).astype(BF16)
    return high, low


def dot(a, b):
    return jnp.dot(a, b, preferred_element_type=F32)


def dot_t(a, b):
    return lax.dot_general(a, b, (((1,), (1,)), ((), ())), preferred_element_type=F32)


def kernel(
    order_ref,
    tiles_ref,
    ids_ref,
    rows_ref,
    times_ref,
    update_ref,
    residual_ref,
    tiles,
    weights,
    ids_in,
    outbox,
    inbox,
    cell_pick,
    cell_sum,
    row_pick,
    row_sum,
    spread,
    prods,
    norm_a,
    norm_b,
    norm_mine,
    load_sem,
    id_send,
    id_recv,
    send_sem,
    recv_sem,
    na_send,
    na_recv,
    nb_send,
    nb_recv,
):
    z, x, y, c = my_place()
    xy = x * 4 + y
    zc = z * 2 + c
    per_load = tiles_ref.shape[0] // LOADS

    def load(i):
        where = pl.ds(i * per_load, per_load)
        return pltpu.make_async_copy(tiles_ref.at[where], tiles.at[where], load_sem.at[i])

    for i in range(LOADS):
        load(i).start()

    barrier = pltpu.get_barrier_semaphore()

    def greet(k, carry):
        pl.semaphore_signal(barrier, inc=1, device_id=partner(k), device_id_type=MESH)
        return carry

    lax.fori_loop(1, DEVICES, greet, 0)
    pl.semaphore_wait(barrier, DEVICES - 1)

    def send_id(k, carry):
        pltpu.make_async_remote_copy(
            src_ref=ids_ref.at[k],
            dst_ref=ids_in.at[k],
            send_sem=id_send,
            recv_sem=id_recv,
            device_id=partner(k),
            device_id_type=MESH,
        ).start()
        return carry

    lax.fori_loop(1, DEVICES, send_id, 0)
    ids_in[0] = ids_ref[0]

    def norm_start(turn, part):
        norm_mine[turn, 0] = part
        norm_a[turn, xy] = part

        def one(d, carry):
            ox = (x + d // 4) % 4
            oy = (y + d % 4) % 4
            pltpu.make_async_remote_copy(
                src_ref=norm_mine.at[turn, 0],
                dst_ref=norm_a.at[turn, xy],
                send_sem=na_send.at[turn],
                recv_sem=na_recv.at[turn],
                device_id=(z, ox * 8 + oy * 2 + c),
                device_id_type=MESH,
            ).start()
            return carry

        lax.fori_loop(1, 16, one, 0)

    def norm_middle(turn):
        got = norm_a.at[turn, pl.ds(0, 15)]
        pltpu.make_async_copy(got, got, na_recv.at[turn]).wait()
        total = norm_a[turn, 0]
        for i in range(1, 16):
            total = total + norm_a[turn, i]
        norm_mine[turn, 1] = total
        norm_b[turn, zc] = total

        def one(d, carry):
            oz = (z + d // 2) % 4
            oc = (c + d % 2) % 2
            pltpu.make_async_remote_copy(
                src_ref=norm_mine.at[turn, 1],
                dst_ref=norm_b.at[turn, zc],
                send_sem=nb_send.at[turn],
                recv_sem=nb_recv.at[turn],
                device_id=(oz, x * 8 + y * 2 + oc),
                device_id_type=MESH,
            ).start()
            return carry

        lax.fori_loop(1, 8, one, 0)

    def norm_end(turn):
        got = norm_b.at[turn, pl.ds(0, 7)]
        pltpu.make_async_copy(got, got, nb_recv.at[turn]).wait()
        total = norm_b[turn, 0]
        for i in range(1, 8):
            total = total + norm_b[turn, i]
        total = total + pltpu.roll(total, 4, 0)
        total = jnp.broadcast_to(jnp.sum(total, axis=1, keepdims=True), total.shape)
        return jnp.sqrt(total + EPSILON)

    def norm_part(values):
        squares = (values * values).reshape(-1, 8, 128)
        return jnp.sum(squares, axis=0)

    def tall(scalar, values):
        return jnp.broadcast_to(scalar[None], (values.shape[0] // 8, 8, 128)).reshape(values.shape)

    def group_send(turn, g, sign):
        def one(k, carry):
            @pl.when(k > 0)
            def _():
                pltpu.make_async_remote_copy(
                    src_ref=outbox.at[turn, k],
                    dst_ref=inbox.at[turn, k],
                    send_sem=send_sem.at[turn],
                    recv_sem=recv_sem.at[turn, g],
                    device_id=partner(k, sign),
                    device_id_type=MESH,
                ).start()

            return carry

        lax.fori_loop(g * GROUP, (g + 1) * GROUP, one, 0)

        @pl.when(g == 0)
        def _():
            inbox[turn, 0] = outbox[turn, 0]

    def group_wait(turn, g):
        @pl.when(g == 0)
        def _():
            got = inbox.at[turn, pl.ds(0, GROUP - 1)]
            pltpu.make_async_copy(got, got, recv_sem.at[turn, 0]).wait()

        @pl.when(g > 0)
        def _():
            got = inbox.at[turn, pl.ds(0, GROUP)]
            pltpu.make_async_copy(got, got, recv_sem.at[turn, g]).wait()

    first_half = (lax.broadcasted_iota(jnp.int32, (16, 128), 0) % 8) < 4
    first_rows = lax.broadcasted_iota(jnp.int32, (8, 128), 0) < 4

    def adjoint_send(turn, ray_vec, build):
        high, low = split(ray_vec)
        zero = jnp.zeros((64, 256), BF16)
        source = jnp.concatenate([jnp.concatenate([high, low], axis=1), zero], axis=0)

        def group(g, carry):
            here = pl.ds(g * 128, 128)
            spread[...] = dot(row_pick[here, :], source)
            for i in range(GROUP):
                k = g * GROUP + i
                if build:
                    for s in range(2):
                        tile = tiles[order_ref[2 * k + s]]
                        tile_high, tile_low = split(tile)
                        weights[k, s * 128 : (s + 1) * 128, 0:128] = tile_high
                        weights[k, s * 128 : (s + 1) * 128, 128:256] = tile_low
                both = jnp.concatenate(
                    [spread[i * 8 : i * 8 + 8, 0:128], spread[i * 8 : i * 8 + 8, 128:256]], axis=0
                )
                left = jnp.concatenate(
                    [jnp.where(first_half, both, 0.0), jnp.where(first_half, 0.0, both)], axis=1
                ).astype(BF16)
                out = dot(left, weights[k])
                out = out[:, 0:128] + out[:, 128:256]
                outbox[turn, k] = out[0:8] + out[8:16]
            group_send(turn, g, 1)

            @pl.when(g == 2)
            def _():
                norm_middle(turn)

            return carry

        lax.fori_loop(0, GROUPS, group, 0)

    def adjoint_finish(turn):
        def group(g, total):
            group_wait(turn, g)
            here = pl.multiple_of(g * 128, 128)
            arrived = inbox[turn, pl.ds(g * GROUP, GROUP)].reshape(128, 128)
            high, low = split(arrived)
            sums = cell_sum[g]
            return total + dot(
                jnp.concatenate([sums, sums], axis=1), jnp.concatenate([high, low], axis=0)
            )

        return lax.fori_loop(0, GROUPS, group, jnp.zeros((128, 128), F32))

    def forward_send(turn, model_vec):
        high, low = split(model_vec)
        source = jnp.concatenate([high, low], axis=0)

        def group(g, carry):
            picks = cell_pick[pl.ds(g * 128, 128), :]
            reply = dot(jnp.concatenate([picks, picks], axis=1), source)
            outbox[turn, pl.ds(g * GROUP, GROUP)] = reply.reshape(GROUP, 8, 128)
            group_send(turn, g, -1)
            return carry

        lax.fori_loop(0, GROUPS, group, 0)

    def forward_finish(turn):
        def group(g, total):
            group_wait(turn, g)
            for i in range(GROUP):
                k = g * GROUP + i
                high, low = split(inbox[turn, k])
                both = jnp.concatenate([high.astype(F32), low.astype(F32)], axis=0)
                left = jnp.concatenate([both, both], axis=1).astype(BF16)
                out = dot_t(left, weights[k])
                out = out[0:8] + out[8:16]
                prods[i * 8 : i * 8 + 8, :] = jnp.where(first_rows, out[:, 0:128], out[:, 128:256])
            high, low = split(prods[...])
            sums = row_sum[g]

            @pl.when(g == 0)
            def _():
                norm_middle(turn)

            return total + dot(
                jnp.concatenate([sums, sums], axis=1), jnp.concatenate([high, low], axis=0)
            )

        return lax.fori_loop(0, GROUPS, group, jnp.zeros((128, 128), F32))[0:64]

    data = jnp.concatenate([times_ref[:, b * 128 : (b + 1) * 128] for b in range(16)], axis=0)

    norm_start(0, norm_part(data))
    lanes = lax.broadcasted_iota(jnp.int32, (128, 128), 1)

    def row_marks(g, carry):
        marks = (rows_ref[pl.ds(g * 128, 128), :] == lanes).astype(F32)
        row_pick[pl.ds(g * 128, 128), :] = marks.astype(BF16)
        row_sum[g] = marks.T.astype(BF16)
        return carry

    lax.fori_loop(0, GROUPS, row_marks, 0)
    for i in range(LOADS):
        load(i).wait()

    adjoint_send(0, data, True)

    got_ids = ids_in.at[pl.ds(0, DEVICES - 1)]
    pltpu.make_async_copy(got_ids, got_ids, id_recv).wait()

    def cell_marks(g, carry):
        marks = ids_in[pl.ds(g * GROUP, GROUP)].reshape(128, 128) == lanes
        marks = marks.astype(F32)
        cell_pick[pl.ds(g * 128, 128), :] = marks.astype(BF16)
        cell_sum[g] = marks.T.astype(BF16)
        return carry

    lax.fori_loop(0, GROUPS, cell_marks, 0)

    pushed = adjoint_finish(0)
    beta_first = norm_end(0)
    ray_vec = data / tall(beta_first, data)
    pushed = pushed / tall(beta_first, pushed)

    norm_start(1, norm_part(pushed))
    forward_send(1, pushed)
    image = forward_finish(1)
    alpha = norm_end(1)
    model_vec = pushed / tall(alpha, pushed)
    direction = model_vec
    phi_bar = beta_first
    rho_bar = alpha
    image = image / tall(alpha, image) - tall(alpha, image) * ray_vec

    norm_start(2, norm_part(image))
    adjoint_send(2, image, False)
    pushed = adjoint_finish(2)
    beta = norm_end(2)
    ray_vec = image / tall(beta, image)
    pushed = pushed / tall(beta, pushed) - tall(beta, pushed) * model_vec

    norm_start(3, norm_part(pushed))
    forward_send(3, pushed)
    rho = jnp.sqrt(rho_bar * rho_bar + beta * beta)
    cosine = rho_bar / rho
    sine = beta / rho
    phi = cosine * phi_bar
    phi_bar = sine * phi_bar
    update = tall(phi / rho, direction) * direction
    image = forward_finish(3)
    alpha = norm_end(3)
    model_vec = pushed / tall(alpha, pushed)
    theta = sine * alpha
    rho_bar = -cosine * alpha
    direction = model_vec - tall(theta / rho, direction) * direction
    image = image / tall(alpha, image) - tall(alpha, image) * ray_vec

    norm_start(4, norm_part(image))
    norm_middle(4)
    beta = norm_end(4)
    rho = jnp.sqrt(rho_bar * rho_bar + beta * beta)
    cosine = rho_bar / rho
    sine = beta / rho
    phi = cosine * phi_bar
    phi_bar = sine * phi_bar
    update = update + tall(phi / rho, direction) * direction
    for b in range(32):
        update_ref[:, b * 128 : (b + 1) * 128] = update[b * 4 : b * 4 + 4, :]
    residual_ref[...] = phi_bar / beta_first

    sent = ids_in.at[pl.ds(0, DEVICES - 1)]
    pltpu.make_async_copy(sent, sent, id_send).wait()
    for turn in range(4):
        sent = outbox.at[turn, pl.ds(0, DEVICES - 1)]
        pltpu.make_async_copy(sent, sent, send_sem.at[turn]).wait()
    for turn in range(NORMS):
        sent = norm_a.at[turn, pl.ds(0, 15)]
        pltpu.make_async_copy(sent, sent, na_send.at[turn]).wait()
        sent = norm_b.at[turn, pl.ds(0, 7)]
        pltpu.make_async_copy(sent, sent, nb_send.at[turn]).wait()


def plan(tile_row, tile_owner, tile_sub, tile_count):
    total = tile_row.shape[0]
    owners = tile_owner[:, 0]
    index = jnp.arange(total, dtype=jnp.int32)
    z, x, y, c = my_place()
    shift = (
        (owners // 32 - z + 4) % 4 * 32
        + ((owners // 8) % 4 - x + 4) % 4 * 8
        + ((owners // 2) % 4 - y + 4) % 4 * 2
        + (owners % 2 - c + 2) % 2
    )
    k = (shift * UNSTRIDE) % DEVICES
    earlier = (owners[:, None] == owners[None, :]) & (index[None, :] < index[:, None])
    rank = jnp.any(earlier, axis=1).astype(jnp.int32)
    position = 2 * k + rank
    hot = index[:, None] == position[None, :]

    def placed(values):
        return jnp.sum(jnp.where(hot, values[None, :], 0), axis=1)

    order = placed(index)
    rhs = jnp.arange(4, dtype=jnp.int32)[None, :]
    ids = placed(tile_sub)[:, None] * 4 + rhs
    rows = placed(jnp.where(index < tile_count[0], tile_row, 1000))[:, None] * 4 + rhs
    ids = jnp.broadcast_to(ids.reshape(DEVICES, 8, 1), (DEVICES, 8, 128))
    rows = jnp.broadcast_to(rows.reshape(total * 4, 1), (total * 4, 128))
    return order, ids, rows


def per_device(tile_values, tile_row, tile_owner, tile_sub, tile_count, residual_times):
    order, ids, rows = plan(tile_row, tile_owner, tile_sub, tile_count)
    vmem = pl.BlockSpec(memory_space=pltpu.VMEM)
    update, residual = pl.pallas_call(
        kernel,
        out_shape=(
            jax.ShapeDtypeStruct((4, 4096), F32),
            jax.ShapeDtypeStruct((8, 128), F32),
        ),
        in_specs=[
            pl.BlockSpec(memory_space=pltpu.SMEM),
            pl.BlockSpec(memory_space=pl.ANY),
            vmem,
            vmem,
            vmem,
        ],
        out_specs=(vmem, vmem),
        scratch_shapes=[
            pltpu.VMEM((256, 128, 128), F32),
            pltpu.VMEM((DEVICES, 256, 256), BF16),
            pltpu.VMEM((DEVICES, 8, 128), jnp.int32),
            pltpu.VMEM((4, DEVICES, 8, 128), F32),
            pltpu.VMEM((4, DEVICES, 8, 128), F32),
            pltpu.VMEM((1024, 128), BF16),
            pltpu.VMEM((GROUPS, 128, 128), BF16),
            pltpu.VMEM((1024, 128), BF16),
            pltpu.VMEM((GROUPS, 128, 128), BF16),
            pltpu.VMEM((128, 256), F32),
            pltpu.VMEM((128, 128), F32),
            pltpu.VMEM((NORMS, 16, 8, 128), F32),
            pltpu.VMEM((NORMS, 8, 8, 128), F32),
            pltpu.VMEM((NORMS, 2, 8, 128), F32),
            pltpu.SemaphoreType.DMA((LOADS,)),
            pltpu.SemaphoreType.DMA,
            pltpu.SemaphoreType.DMA,
            pltpu.SemaphoreType.DMA((4,)),
            pltpu.SemaphoreType.DMA((4, GROUPS)),
            pltpu.SemaphoreType.DMA((NORMS,)),
            pltpu.SemaphoreType.DMA((NORMS,)),
            pltpu.SemaphoreType.DMA((NORMS,)),
            pltpu.SemaphoreType.DMA((NORMS,)),
        ],
        compiler_params=pltpu.CompilerParams(
            collective_id=0, has_side_effects=True, vmem_limit_bytes=52 * 2**20
        ),
        name="lsqr",
    )(order, tile_values, ids, rows, residual_times)
    return update, residual[0:4, 0]


def solution(mesh):
    placed = (
        P(("region", "rays"), None, None),
        P(("region", "rays")),
        P(("region", "rays"), None),
        P(("region", "rays")),
        P(("region", "rays")),
        P(None, ("region", "rays")),
    )
    return jax.shard_map(
        per_device,
        mesh=mesh,
        in_specs=placed,
        out_specs=(P(None, ("region", "rays")), P()),
        check_vma=False,
    )
```

time: 545 us -> 99.6 us (0.18)
  blocking collectives: 355 us -> 0 us
  matrix products: 94.9 us -> 0 us
  Pallas kernels: 0 us -> 91.6 us
  local copies, waits for them, and re-layouts: 40.2 us -> 2.92 us
  waiting for transfers between devices: 25.5 us -> 0 us
  starting transfers between devices: 21 us -> 0 us
    psum x5 -> x0, blocking collectives: 320 us -> none  [the longest x3 193 us: ray_norm(): return jnp.sqrt(lax.psum(squares(values), ('region', 'rays')) + EPSILON)]
    dot_general x12 -> x0, matrix products: 94.9 us -> none  [the longest x2 57.4 us: per_device(): jnp.einsum('trc,tnc->tnr', tile_values, picked, precision=PRECISE)]
    pallas_call x0 -> x1, Pallas kernels: none -> 91.6 us  [per_device(): pl.pallas_call(kernel, out_shape=(jax.ShapeDtypeStruct((4, 4096), F32), j...]
    all_to_all x2 -> x0, blocking collectives: 35.9 us -> none  [the longest x1 17.9 us: per_device(): lax.all_to_all(reply_rows, ('region', 'rays'), split_axis=0, concat_axis=...]
    scatter x3 -> x0, local copies, waits for them, and re-layouts: 32.9 us -> none  [the longest x2 31.3 us: adjoint_terms(): return jnp.zeros((capacity,) + contribution.shape[1:], jnp.float32).at[po...]
    all_to_all x3 -> x0, waiting for transfers between devices: 25.5 us -> none  [the longest x1 13.5 us: per_device(): lax.all_to_all(reply_rows, ('region', 'rays'), split_axis=0, concat_axis=...]
    all_to_all x3 -> x0, starting transfers between devices: 21 us -> none  [the longest x1 11.5 us: per_device(): lax.all_to_all(request_ids, ('region', 'rays'), split_axis=0, concat_axis...]
  transfers between devices with their start and end apart: 3 -> 0, of which waited for: 2 -> 0; matrix products, arithmetic and copies ran while one was open for 8% -> 0% of each run, Pallas kernels for 0% -> 0%
where the time goes in v1:
time: 99.6 us; the launch traced here: 99.3 us
  Pallas kernels  91.6 us (92%)
  other arithmetic  3.4 us (3%)
  local copies, waits for them, and re-layouts  2.92 us (3%)
  between operations  1.39 us (1%)
    pallas_call x1, Pallas kernels, per_device(): pl.pallas_call(kernel, out_shape=(jax.ShapeDtypeStruct((4, 4096), F32), j...  91.6 us

profile of v1, /device:TPU:1, one launch (start us, length us, event | category | flops | bytes accessed | tf_op | source)
XLA Modules:
  0.0 99.3 jit_solution(1782624536389461845)
XLA Ops:
  1.3 0.7 compare_select_fusion.14
  2.0 0.9 fusion.1
  2.9 0.7 fusion.14
  3.7 0.1 add.210
  3.8 0.9 select_reduce_fusion
  4.6 0.1 mul.66
  4.8 0.1 copy.10
  4.9 0.1 broadcast_add_fusion
  4.9 0.1 copy.11
  5.0 0.1 iota_add_fusion
  5.2 0.1 add.216
  5.3 0.2 broadcast_in_dim.48.ids_ref
  5.5 0.2 broadcast_in_dim.51.rows_ref
  5.7 0.0 copy-start
  5.7 0.8 copy-done
  6.4 91.6 %lsqr.1 = (f32[4,4096]{1,0:T(4,128)S(1)}, f32[8,128]{1,0:T(8,128)S(1)}) custom-call(s32[256]{0:T(256)S(1)} %get-tuple-element.8.order_ref, f32[256,128,128]{2,1,0:T(8,128)} %tiles_ref.1, s32[128,8,128]{2,1,0:T(8,128)S(1)} %broadcast_in_dim.48.ids_ref, s32[1024,128]{1,0:T(8,128)S(1)} %broadcast_in_dim.51.rows_ref, f32[4,2048]{1,0:T(4,128)S(1)} %copy-done), custom_call_target="tpu_custom_call" | custom-call | tf_op jit(solution)/shard_map/lsqr/pallas_call | solution.py:425
  98.1 0.6 slice_reduce_fusion
  98.7 0.6 copy.14
  (3 shorter events, 0.0 us)
Async XLA Ops:
  5.7 0.8 copy-start

commit v2 on v1

--- a/solution.py
+++ b/solution.py
@@ -15,8 +15,6 @@
 DEVICES = 128
 GROUP = 16
 GROUPS = DEVICES // GROUP
-STRIDE = 37
-UNSTRIDE = pow(STRIDE, -1, DEVICES)
 NORMS = 5
 LOADS = 8
 
@@ -27,14 +25,18 @@
     return z, rays // 8, (rays // 2) % 4, rays % 2
 
 
-def partner(k, sign=1):
+def corners(sign):
     z, x, y, c = my_place()
-    shift = (k * STRIDE) % DEVICES
-    oz = (z + 4 + sign * (shift // 32)) % 4
-    ox = (x + 4 + sign * ((shift // 8) % 4)) % 4
-    oy = (y + 4 + sign * ((shift // 2) % 4)) % 4
-    oc = (c + shift % 2) % 2
-    return (oz, ox * 8 + oy * 2 + oc)
+    xs = [((x + 4 + sign * d) % 4) * 8 for d in range(4)]
+    ys = [((y + 4 + sign * d) % 4) * 2 for d in range(4)]
+    return [xs[i // 4] + ys[i % 4] for i in range(GROUP)]
+
+
+def group_partners(g, plane, sign):
+    z, x, y, c = my_place()
+    zs = [(z + 4 + sign * ((g // 2 + d) % 4)) % 4 for d in range(4)]
+    cs = [(c + g + d) % 2 for d in range(2)]
+    return [(zs[i % 4], plane[i] + cs[(i // 4) % 2]) for i in range(GROUP)]
 
 
 def split(values):
@@ -97,45 +99,56 @@
 
     barrier = pltpu.get_barrier_semaphore()
 
-    def greet(k, carry):
-        pl.semaphore_signal(barrier, inc=1, device_id=partner(k), device_id_type=MESH)
-        return carry
-
-    lax.fori_loop(1, DEVICES, greet, 0)
-    pl.semaphore_wait(barrier, DEVICES - 1)
-
-    def send_id(k, carry):
+    planes = {1: corners(1), -1: corners(-1)}
+
+    def each_partner(g, sign, action):
+        for i, device in enumerate(group_partners(g, planes[sign], sign)):
+            if i == 0:
+
+                @pl.when(g > 0)
+                def _():
+                    action(g * GROUP, device)
+            else:
+                action(g * GROUP + i, device)
+
+    def greet(k, device):
+        pl.semaphore_signal(barrier, inc=1, device_id=device, device_id_type=MESH)
+
+    def send_id(k, device):
         pltpu.make_async_remote_copy(
             src_ref=ids_ref.at[k],
             dst_ref=ids_in.at[k],
             send_sem=id_send,
             recv_sem=id_recv,
-            device_id=partner(k),
+            device_id=device,
             device_id_type=MESH,
         ).start()
-        return carry
-
-    lax.fori_loop(1, DEVICES, send_id, 0)
+
+    def all_partners(action):
+        def group(g, carry):
+            each_partner(g, 1, action)
+            return carry
+
+        lax.fori_loop(0, GROUPS, group, 0)
+
+    all_partners(greet)
+    pl.semaphore_wait(barrier, DEVICES - 1)
+    all_partners(send_id)
     ids_in[0] = ids_ref[0]
 
     def norm_start(turn, part):
         norm_mine[turn, 0] = part
         norm_a[turn, xy] = part
 
-        def one(d, carry):
-            ox = (x + d // 4) % 4
-            oy = (y + d % 4) % 4
+        for d in range(1, 16):
             pltpu.make_async_remote_copy(
                 src_ref=norm_mine.at[turn, 0],
                 dst_ref=norm_a.at[turn, xy],
                 send_sem=na_send.at[turn],
                 recv_sem=na_recv.at[turn],
-                device_id=(z, ox * 8 + oy * 2 + c),
+                device_id=(z, planes[1][d] + c),
                 device_id_type=MESH,
             ).start()
-            return carry
-
-        lax.fori_loop(1, 16, one, 0)
 
     def norm_middle(turn):
         got = norm_a.at[turn, pl.ds(0, 15)]
@@ -146,20 +159,15 @@
         norm_mine[turn, 1] = total
         norm_b[turn, zc] = total
 
-        def one(d, carry):
-            oz = (z + d // 2) % 4
-            oc = (c + d % 2) % 2
+        for d in range(1, 8):
             pltpu.make_async_remote_copy(
                 src_ref=norm_mine.at[turn, 1],
                 dst_ref=norm_b.at[turn, zc],
                 send_sem=nb_send.at[turn],
                 recv_sem=nb_recv.at[turn],
-                device_id=(oz, x * 8 + y * 2 + oc),
+                device_id=((z + d // 2) % 4, planes[1][0] + (c + d) % 2),
                 device_id_type=MESH,
             ).start()
-            return carry
-
-        lax.fori_loop(1, 8, one, 0)
 
     def norm_end(turn):
         got = norm_b.at[turn, pl.ds(0, 7)]
@@ -179,21 +187,17 @@
         return jnp.broadcast_to(scalar[None], (values.shape[0] // 8, 8, 128)).reshape(values.shape)
 
     def group_send(turn, g, sign):
-        def one(k, carry):
-            @pl.when(k > 0)
-            def _():
-                pltpu.make_async_remote_copy(
-                    src_ref=outbox.at[turn, k],
-                    dst_ref=inbox.at[turn, k],
-                    send_sem=send_sem.at[turn],
-                    recv_sem=recv_sem.at[turn, g],
-                    device_id=partner(k, sign),
-                    device_id_type=MESH,
-                ).start()
-
-            return carry
-
-        lax.fori_loop(g * GROUP, (g + 1) * GROUP, one, 0)
+        def one(k, device):
+            pltpu.make_async_remote_copy(
+                src_ref=outbox.at[turn, k],
+                dst_ref=inbox.at[turn, k],
+                send_sem=send_sem.at[turn],
+                recv_sem=recv_sem.at[turn, g],
+                device_id=device,
+                device_id_type=MESH,
+            ).start()
+
+        each_partner(g, sign, one)
 
         @pl.when(g == 0)
         def _():
@@ -395,13 +399,10 @@
     owners = tile_owner[:, 0]
     index = jnp.arange(total, dtype=jnp.int32)
     z, x, y, c = my_place()
-    shift = (
-        (owners // 32 - z + 4) % 4 * 32
-        + ((owners // 8) % 4 - x + 4) % 4 * 8
-        + ((owners // 2) % 4 - y + 4) % 4 * 2
-        + (owners % 2 - c + 2) % 2
-    )
-    k = (shift * UNSTRIDE) % DEVICES
+    dz, dx = (owners // 32 - z + 4) % 4, ((owners // 8) % 4 - x + 4) % 4
+    dy, dc = ((owners // 2) % 4 - y + 4) % 4, (owners % 2 - c + 2) % 2
+    g = (dz - dy + 4) % 4 * 2 + (dc + dx) % 2
+    k = g * GROUP + dx * 4 + dy
     earlier = (owners[:, None] == owners[None, :]) & (index[None, :] < index[:, None])
     rank = jnp.any(earlier, axis=1).astype(jnp.int32)
     position = 2 * k + rank

time: 99.6 us -> 89.7 us (0.901)
  Pallas kernels: 91.6 us -> 81.7 us
    pallas_call x1, Pallas kernels: 91.6 us -> 81.7 us  [per_device(): pl.pallas_call(kernel, out_shape=(jax.ShapeDtypeStruct((4, 4096), F32), j...]
where the time goes in v2:
time: 89.7 us; the launch traced here: 89.4 us
  Pallas kernels  81.7 us (91%)
  other arithmetic  3.41 us (4%)
  local copies, waits for them, and re-layouts  2.92 us (3%)
  between operations  1.39 us (2%)
    pallas_call x1, Pallas kernels, per_device(): pl.pallas_call(kernel, out_shape=(jax.ShapeDtypeStruct((4, 4096), F32), j...  81.7 us

profile of v2, /device:TPU:1, one launch (start us, length us, event | category | flops | bytes accessed | tf_op | source)
XLA Modules:
  0.0 89.4 jit_solution(1895622365314010430)
XLA Ops:
  1.3 0.7 compare_select_fusion.16
  2.0 0.9 %fusion.1 = pred[256]{0:T(512)(128)(4,1)S(1)} fusion(s32[256]{0:T(256)} %bitcast.7), kind=kLoop, calls=%fused_computation.6 | loop fusion | flops 261888 | bytes 1280 | tf_op jit(solution)/shard_map/reduce_or | solution.py:407
  2.9 0.7 convert_add_fusion
  3.7 0.1 add.235
  3.8 0.9 select_reduce_fusion
  4.6 0.1 mul.56
  4.8 0.1 copy.10
  4.9 0.1 broadcast_add_fusion
  4.9 0.1 copy.11
  5.1 0.1 iota_add_fusion
  5.2 0.1 add.241
  5.3 0.2 broadcast_in_dim.48.ids_ref
  5.5 0.2 broadcast_in_dim.51.rows_ref
  5.7 0.0 copy-start
  5.7 0.8 copy-done
  6.4 81.7 %lsqr.1 = (f32[4,4096]{1,0:T(4,128)S(1)}, f32[8,128]{1,0:T(8,128)S(1)}) custom-call(s32[256]{0:T(256)S(1)} %get-tuple-element.8.order_ref, f32[256,128,128]{2,1,0:T(8,128)} %tiles_ref.1, s32[128,8,128]{2,1,0:T(8,128)S(1)} %broadcast_in_dim.48.ids_ref, s32[1024,128]{1,0:T(8,128)S(1)} %broadcast_in_dim.51.rows_ref, f32[4,2048]{1,0:T(4,128)S(1)} %copy-done), custom_call_target="tpu_custom_call" | custom-call | tf_op jit(solution)/shard_map/lsqr/pallas_call | solution.py:426
  88.2 0.6 slice_reduce_fusion
  88.8 0.6 copy.14
  (3 shorter events, 0.0 us)
Async XLA Ops:
  5.7 0.8 copy-start

commit v3 on v2

v3 whole, which is shorter than its diff:
```python
import functools

import jax
import jax.numpy as jnp
from jax import lax
from jax.experimental import pallas as pl
from jax.experimental.pallas import tpu as pltpu
from jax.sharding import PartitionSpec as P

EPSILON = 1e-06
MESH = pl.DeviceIdType.MESH
F32 = jnp.float32
BF16 = jnp.bfloat16

DEVICES = 128
GROUP = 16
GROUPS = DEVICES // GROUP
def distance(shift):
    hops = [shift // 32, shift // 8 % 4, shift // 2 % 4]
    return sum(min(d, 4 - d) for d in hops)


ORDER = sorted(range(DEVICES), key=lambda shift: (-distance(shift), -(shift % 2), shift))
OWN = DEVICES - 1
FORWARD_SENDS = (0, 7, 1, 6, 2, 5, 3, 4)
FORWARD_TURNS = (7, 0, 6, 1, 5, 2, 4, 3)
NORMS = 5
CHUNKS = 2
LOADS = 8


def my_place():
    z = lax.axis_index("region")
    rays = lax.axis_index("rays")
    return z, rays // 8, (rays // 2) % 4, rays % 2


def partners(sign):
    z, x, y, c = my_place()
    zs = [(z + 4 + sign * d) % 4 for d in range(4)]
    xs = [((x + 4 + sign * d) % 4) * 8 for d in range(4)]
    ys = [((y + 4 + sign * d) % 4) * 2 for d in range(4)]
    cs = [c, (c + 1) % 2]
    rays = [xs[r // 8] + ys[r // 2 % 4] + cs[r % 2] for r in range(32)]
    return [(zs[shift // 32], rays[shift % 32]) for shift in ORDER]


def split(values):
    high = values.astype(BF16)
    low = (values - high.astype(F32)).astype(BF16)
    return high, low


def dot(a, b):
    return jnp.dot(a, b, preferred_element_type=F32)


def dot_t(a, b):
    return lax.dot_general(a, b, (((1,), (1,)), ((), ())), preferred_element_type=F32)


def kernel(
    count_ref,
    tiles_ref,
    row_ref,
    owner_ref,
    sub_ref,
    times_ref,
    update_ref,
    residual_ref,
    tiles,
    weights,
    order_row,
    order,
    ids_mine,
    ids_in,
    outbox,
    inbox,
    cell_pick,
    cell_sum,
    row_pick,
    row_sum,
    spread,
    prods,
    norm_in,
    norm_mine,
    load_sem,
    order_sem,
    id_send,
    id_recv,
    send_sem,
    recv_sem,
    norm_send,
    norm_recv,
):
    z, x, y, c = my_place()
    me = z * 32 + x * 8 + y * 2 + c
    per_load = tiles_ref.shape[0] // LOADS

    def load(i):
        where = pl.ds(i * per_load, per_load)
        return pltpu.make_async_copy(tiles_ref.at[where], tiles.at[where], load_sem.at[i])

    for i in range(LOADS):
        load(i).start()

    barrier = pltpu.get_barrier_semaphore()

    devices = {1: partners(1), -1: partners(-1)}

    def greet(k, device):
        pl.semaphore_signal(barrier, inc=1, device_id=device, device_id_type=MESH)

    def send_id(k, device):
        pltpu.make_async_remote_copy(
            src_ref=ids_mine.at[k],
            dst_ref=ids_in.at[k],
            send_sem=id_send,
            recv_sem=id_recv,
            device_id=device,
            device_id_type=MESH,
        ).start()

    def all_partners(action):
        for k in range(DEVICES - 1):
            action(k, devices[1][k])

    all_partners(greet)

    sublane = lax.broadcasted_iota(jnp.int32, (8, 128), 0)
    lane = lax.broadcasted_iota(jnp.int32, (8, 128), 1)

    def norm_start(turn, part):
        total = jnp.broadcast_to(jnp.sum(part, axis=1, keepdims=True), (8, 128))
        row = jnp.sum(jnp.where(lane % 8 == sublane, total, 0.0), axis=0, keepdims=True)
        norm_mine[turn] = row
        norm_in[turn, me] = row

    def send_norm(turn, device):
        pltpu.make_async_remote_copy(
            src_ref=norm_mine.at[turn],
            dst_ref=norm_in.at[turn, me],
            send_sem=norm_send.at[turn],
            recv_sem=norm_recv.at[turn],
            device_id=device,
            device_id_type=MESH,
        ).start()

    def norm_end(turn):
        got = norm_in.at[turn, pl.ds(0, DEVICES - 1)]
        pltpu.make_async_copy(got, got, norm_recv.at[turn]).wait()
        row = jnp.sum(norm_in[turn], axis=0)
        mine = (lane < 8) & (lane % 4 == sublane % 4)
        total = jnp.sum(
            jnp.where(mine, jnp.broadcast_to(row, (8, 128)), 0.0), axis=1, keepdims=True
        )
        return jnp.sqrt(jnp.broadcast_to(total, (8, 128)) + EPSILON)

    def norm_part(values):
        squares = (values * values).reshape(-1, 8, 128)
        return jnp.sum(squares, axis=0)

    def tall(scalar, values):
        return jnp.broadcast_to(scalar[None], (values.shape[0] // 8, 8, 128)).reshape(values.shape)

    def group_send(turn, g, sign):
        def one(k, device):
            send_norm(turn, device)
            if turn == 0:
                send_id(k, device)
            pltpu.make_async_remote_copy(
                src_ref=outbox.at[turn, k],
                dst_ref=inbox.at[turn, k],
                send_sem=send_sem.at[turn],
                recv_sem=recv_sem.at[turn, g],
                device_id=device,
                device_id_type=MESH,
            ).start()

        for k in range(g * GROUP, (g + 1) * GROUP):
            if k != OWN:
                one(k, devices[sign][k])

        if g == GROUPS - 1:
            inbox[turn, OWN] = outbox[turn, OWN]

    def group_wait(turn, g):
        got = inbox.at[turn, pl.ds(0, GROUP - 1 if g == GROUPS - 1 else GROUP)]
        pltpu.make_async_copy(got, got, recv_sem.at[turn, g]).wait()

    first_half = (lax.broadcasted_iota(jnp.int32, (16, 128), 0) % 8) < 4
    first_rows = lax.broadcasted_iota(jnp.int32, (8, 128), 0) < 4

    def adjoint_send(turn, ray_vec, build):
        high, low = split(ray_vec)
        zero = jnp.zeros((64, 256), BF16)
        source = jnp.concatenate([jnp.concatenate([high, low], axis=1), zero], axis=0)

        spread[...] = dot(row_pick[...], source)

        def group(g):
            for i in range(GROUP):
                k = g * GROUP + i
                if build:
                    for s in range(2):
                        tile = tiles[order[0, 2 * k + s]]
                        tile_high, tile_low = split(tile)
                        weights[k, s * 128 : (s + 1) * 128, 0:128] = tile_high
                        weights[k, s * 128 : (s + 1) * 128, 128:256] = tile_low
                both = jnp.concatenate(
                    [spread[pl.ds(k * 8, 8), 0:128], spread[pl.ds(k * 8, 8), 128:256]], axis=0
                )
                left = jnp.concatenate(
                    [jnp.where(first_half, both, 0.0), jnp.where(first_half, 0.0, both)], axis=1
                ).astype(BF16)
                out = dot(left, weights[k])
                out = out[:, 0:128] + out[:, 128:256]
                outbox[turn, k] = out[0:8] + out[8:16]

        for g in range(GROUPS):
            group(g)
            if build and g == 0:
                pl.semaphore_wait(barrier, DEVICES - 1)
            group_send(turn, g, 1)

    def adjoint_finish(turn):
        total = jnp.zeros((128, 128), F32)
        for chunk in range(CHUNKS):
            first = chunk * GROUPS // CHUNKS
            for g in range(first, first + GROUPS // CHUNKS):
                group_wait(turn, g)
            arrived = inbox[turn, first * GROUP : (first + GROUPS // CHUNKS) * GROUP]
            high, low = split(arrived.reshape(-1, 128))
            sums = cell_sum[:, first * 128 : (first + GROUPS // CHUNKS) * 128]
            total = total + dot(sums, high) + dot(sums, low)
        return total

    def forward_send(turn, model_vec):
        high, low = split(model_vec)
        source = jnp.concatenate([high, low], axis=0)

        picks = cell_pick[...]
        reply = dot(jnp.concatenate([picks, picks], axis=1), source)
        outbox[turn] = reply.reshape(DEVICES, 8, 128)

        for g in FORWARD_SENDS:
            group_send(turn, g, -1)

    def forward_finish(turn):
        for g in FORWARD_TURNS:
            group_wait(turn, g)
            for i in range(GROUP):
                k = g * GROUP + i
                arrived = inbox[turn, k]
                high = arrived.astype(BF16).astype(F32)
                both = jnp.concatenate([high, arrived - high], axis=0)
                left = jnp.concatenate([both, both], axis=1).astype(BF16)
                out = dot_t(left, weights[k])
                out = out[0:8] + out[8:16]
                prods[pl.ds(k * 8, 8), :] = jnp.where(first_rows, out[:, 0:128], out[:, 128:256])
        high, low = split(prods[...])
        sums = row_sum[...]
        return dot(sums, high) + dot(sums, low)

    data = jnp.concatenate([times_ref[:, b * 128 : (b + 1) * 128] for b in range(16)], axis=0)

    norm_start(0, norm_part(data))
    lanes = lax.broadcasted_iota(jnp.int32, (128, 128), 1)

    owner = owner_ref[...]
    shift = (
        (((owner >> 5) - z) & 3) * 32
        + (((owner >> 3) - x) & 3) * 8
        + (((owner >> 1) - y) & 3) * 2
        + ((owner - c) & 1)
    )
    tile_lane = lax.broadcasted_iota(jnp.int32, (128, 256), 1)
    tile_sublane = lax.broadcasted_iota(jnp.int32, (128, 256), 0)

    def upright(row, half):
        column = jnp.broadcast_to(row[:, half * 128 : half * 128 + 128], (128, 128)).T
        return jnp.concatenate([column, column], axis=1)

    rank = jnp.zeros((1, 256), jnp.int32)
    for half in range(2):
        earlier = (upright(owner, half) == owner) & (tile_sublane + half * 128 < tile_lane)
        rank = rank + jnp.sum(earlier.astype(jnp.int32), axis=0, keepdims=True)
    code = shift * 2 + rank
    lane_row = tile_lane[0:1]
    keys = jnp.zeros((1, 256), jnp.int32)
    for k in range(DEVICES):
        keys = jnp.where(lane_row >> 1 == k, ORDER[k] * 2, keys)
    keys = keys + (lane_row & 1)
    found = jnp.zeros((1, 256), jnp.int32)
    for half in range(2):
        hit = upright(code, half) == keys
        found = found + jnp.sum(
            jnp.where(hit, tile_sublane + half * 128, 0), axis=0, keepdims=True
        )
    order_row[...] = found
    to_scalars = pltpu.make_async_copy(order_row, order, order_sem)
    to_scalars.start()

    live_row = jnp.where(lane_row < count_ref[0], row_ref[...], 31)
    payload = (live_row + 32 * sub_ref[...]).astype(F32)
    slot = lax.broadcasted_iota(jnp.int32, (8, 256), 0) >> 2
    for g in range(GROUPS):
        for i in range(GROUP):
            k = g * GROUP + i
            hit = code == slot + 2 * ORDER[k]
            value = jnp.sum(jnp.where(hit, payload, 0.0), axis=1, keepdims=True)
            value = jnp.broadcast_to(value, (8, 128)).astype(jnp.int32)
            marks = ((value & 31) * 4 + (sublane & 3) == lane).astype(F32)
            spread[i * 8 : i * 8 + 8, 0:128] = marks
            cells = (value >> 5 == lane >> 2).astype(jnp.int32)
            ids_mine[k] = cells[0:1] + 2 * cells[4:5]
        marks = spread[0:128, 0:128]
        row_pick[g * 128 : g * 128 + 128, :] = marks.astype(BF16)
        row_sum[:, g * 128 : g * 128 + 128] = marks.T[0:64].astype(BF16)
    ids_in[OWN] = ids_mine[OWN]
    to_scalars.wait()
    for i in range(LOADS):
        load(i).wait()

    adjoint_send(0, data, True)

    got_ids = ids_in.at[pl.ds(0, DEVICES - 1)]
    pltpu.make_async_copy(got_ids, got_ids, id_recv).wait()

    def cell_marks(g, carry):
        for i in range(GROUP):
            code = jnp.broadcast_to(ids_in[g * GROUP + i], (8, 128))
            hit = (code == sublane // 4 + 1) | (code == 3)
            marks = (hit & (lane % 4 == sublane % 4)).astype(F32)
            spread[i * 8 : i * 8 + 8, 0:128] = marks
        marks = spread[0:128, 0:128]
        cell_pick[pl.ds(g * 128, 128), :] = marks.astype(BF16)
        cell_sum[:, pl.ds(pl.multiple_of(g * 128, 128), 128)] = marks.T.astype(BF16)
        return carry

    lax.fori_loop(0, GROUPS, cell_marks, 0)

    pushed = adjoint_finish(0)
    beta_first = norm_end(0)
    ray_vec = data / tall(beta_first, data)
    pushed = pushed / tall(beta_first, pushed)

    norm_start(1, norm_part(pushed))
    forward_send(1, pushed)
    image = forward_finish(1)
    alpha = norm_end(1)
    model_vec = pushed / tall(alpha, pushed)
    direction = model_vec
    phi_bar = beta_first
    rho_bar = alpha
    image = image / tall(alpha, image) - tall(alpha, image) * ray_vec

    norm_start(2, norm_part(image))
    adjoint_send(2, image, False)
    pushed = adjoint_finish(2)
    beta = norm_end(2)
    ray_vec = image / tall(beta, image)
    pushed = pushed / tall(beta, pushed) - tall(beta, pushed) * model_vec

    norm_start(3, norm_part(pushed))
    forward_send(3, pushed)
    rho = jnp.sqrt(rho_bar * rho_bar + beta * beta)
    cosine = rho_bar / rho
    sine = beta / rho
    phi = cosine * phi_bar
    phi_bar = sine * phi_bar
    update = tall(phi / rho, direction) * direction
    image = forward_finish(3)
    alpha = norm_end(3)
    model_vec = pushed / tall(alpha, pushed)
    theta = sine * alpha
    rho_bar = -cosine * alpha
    direction = model_vec - tall(theta / rho, direction) * direction
    image = image / tall(alpha, image) - tall(alpha, image) * ray_vec

    norm_start(4, norm_part(image))
    all_partners(lambda k, device: send_norm(4, device))
    beta = norm_end(4)
    rho = jnp.sqrt(rho_bar * rho_bar + beta * beta)
    cosine = rho_bar / rho
    sine = beta / rho
    phi = cosine * phi_bar
    phi_bar = sine * phi_bar
    update = update + tall(phi / rho, direction) * direction
    for b in range(32):
        update_ref[:, b * 128 : (b + 1) * 128] = update[b * 4 : b * 4 + 4, :]
    residual_ref[...] = phi_bar / beta_first

    sent = ids_in.at[pl.ds(0, DEVICES - 1)]
    pltpu.make_async_copy(sent, sent, id_send).wait()
    for turn in range(4):
        sent = outbox.at[turn, pl.ds(0, DEVICES - 1)]
        pltpu.make_async_copy(sent, sent, send_sem.at[turn]).wait()
    for turn in range(NORMS):
        sent = norm_in.at[turn, pl.ds(0, DEVICES - 1)]
        pltpu.make_async_copy(sent, sent, norm_send.at[turn]).wait()


def per_device(tile_values, tile_row, tile_owner, tile_sub, tile_count, residual_times):
    tiles = tile_row.shape[0]
    vmem = pl.BlockSpec(memory_space=pltpu.VMEM)
    update, residual = pl.pallas_call(
        kernel,
        out_shape=(
            jax.ShapeDtypeStruct((4, 4096), F32),
            jax.ShapeDtypeStruct((8, 128), F32),
        ),
        in_specs=[
            pl.BlockSpec(memory_space=pltpu.SMEM),
            pl.BlockSpec(memory_space=pl.ANY),
            vmem,
            vmem,
            vmem,
            vmem,
        ],
        out_specs=(vmem, vmem),
        scratch_shapes=[
            pltpu.VMEM((256, 128, 128), F32),
            pltpu.VMEM((DEVICES, 256, 256), BF16),
            pltpu.VMEM((1, 256), jnp.int32),
            pltpu.SMEM((1, 256), jnp.int32),
            pltpu.VMEM((DEVICES, 1, 128), jnp.int32),
            pltpu.VMEM((DEVICES, 1, 128), jnp.int32),
            pltpu.VMEM((4, DEVICES, 8, 128), F32),
            pltpu.VMEM((4, DEVICES, 8, 128), F32),
            pltpu.VMEM((1024, 128), BF16),
            pltpu.VMEM((128, 1024), BF16),
            pltpu.VMEM((1024, 128), BF16),
            pltpu.VMEM((64, 1024), BF16),
            pltpu.VMEM((1024, 256), F32),
            pltpu.VMEM((1024, 128), F32),
            pltpu.VMEM((NORMS, DEVICES, 1, 128), F32),
            pltpu.VMEM((NORMS, 1, 128), F32),
            pltpu.SemaphoreType.DMA((LOADS,)),
            pltpu.SemaphoreType.DMA,
            pltpu.SemaphoreType.DMA,
            pltpu.SemaphoreType.DMA,
            pltpu.SemaphoreType.DMA((4,)),
            pltpu.SemaphoreType.DMA((4, GROUPS)),
            pltpu.SemaphoreType.DMA((NORMS,)),
            pltpu.SemaphoreType.DMA((NORMS,)),
        ],
        compiler_params=pltpu.CompilerParams(
            collective_id=0, has_side_effects=True, vmem_limit_bytes=52 * 2**20
        ),
        name="lsqr",
    )(
        tile_count,
        tile_values,
        tile_row.reshape(1, tiles),
        tile_owner.reshape(1, tiles),
        tile_sub.reshape(1, tiles),
        residual_times,
    )
    return update, residual[0:4, 0]


def solution(mesh):
    placed = (
        P(("region", "rays"), None, None),
        P(("region", "rays")),
        P(("region", "rays"), None),
        P(("region", "rays")),
        P(("region", "rays")),
        P(None, ("region", "rays")),
    )
    return jax.shard_map(
        per_device,
        mesh=mesh,
        in_specs=placed,
        out_specs=(P(None, ("region", "rays")), P()),
        check_vma=False,
    )
```

time: 89.7 us -> 74.1 us (0.83)
  Pallas kernels: 81.7 us -> 68.5 us
  other arithmetic: 3.41 us -> 0 us
  local copies, waits for them, and re-layouts: 2.92 us -> 4.04 us
    pallas_call x1, Pallas kernels: 81.7 us -> 68.5 us  [per_device(): pl.pallas_call(kernel, out_shape=(jax.ShapeDtypeStruct((4, 4096), F32), j...]
    unnamed x3 -> x9, local copies, waits for them, and re-layouts: 1.39 us -> 3.42 us
    reduce_or x1 -> x0, other arithmetic: 0.93 us -> none  [plan(): rank = jnp.any(earlier, axis=1).astype(jnp.int32)]
    add x3 -> x0, other arithmetic: 0.9 us -> none  [the longest x1 0.73 us: plan(): position = 2 * k + rank]
where the time goes in v3:
time: 74.1 us; the launch traced here: 73.8 us
  Pallas kernels  68.5 us (92%)
  local copies, waits for them, and re-layouts  4.04 us (5%)
  between operations  1.3 us (2%)
    pallas_call x1, Pallas kernels, per_device(): pl.pallas_call(kernel, out_shape=(jax.ShapeDtypeStruct((4, 4096), F32), j...  68.5 us
    unnamed x9, local copies, waits for them, and re-layouts  3.42 us

profile of v3, /device:TPU:1, one launch (start us, length us, event | category | flops | bytes accessed | tf_op | source)
XLA Modules:
  0.0 73.8 jit_solution(11073868300586572270)
XLA Ops:
  1.3 0.0 copy-start
  1.3 0.7 %copy-done = f32[4,2048]{1,0:T(4,128)S(1)} copy-done((f32[4,2048]{1,0:T(4,128)S(1)}, f32[4,2048]{1,0:T(4,128)}, u32[]{:S(2)}) %copy-start) | copy-done | bytes 32792
  2.0 0.0 copy-start.1
  2.0 0.7 copy-done.1
  2.7 0.0 copy-start.2
  2.7 0.7 copy-done.2
  3.4 0.0 copy-start.3
  3.4 0.7 copy-done.3
  4.1 68.5 %lsqr.1 = (f32[4,4096]{1,0:T(4,128)S(1)}, f32[8,128]{1,0:T(8,128)S(1)}) custom-call(s32[1]{0:T(128)S(6)} %copy.9.count_ref, f32[256,128,128]{2,1,0:T(8,128)} %tiles_ref.1, s32[1,256]{1,0:T(1,128)S(1)} %bitcast.3, s32[1,256]{1,0:T(1,128)S(1)} %bitcast.4, s32[1,256]{1,0:T(1,128)S(1)} %bitcast.5, f32[4,2048]{1,0:T(4,128)S(1)} %copy-done), custom_call_target="tpu_custom_call" | custom-call | tf_op jit(solution)/shard_map/lsqr/pallas_call | solution.py:407
  72.6 0.6 slice_reduce_fusion
  73.2 0.6 copy.10
Async XLA Ops:
  1.3 0.8 %copy-start = (f32[4,2048]{1,0:T(4,128)S(1)}, f32[4,2048]{1,0:T(4,128)}, u32[]{:S(2)}) copy-start(f32[4,2048]{1,0:T(4,128)} %times_ref.1) | copy-start | bytes 98308
  2.0 0.7 copy-start.1
  2.7 0.7 copy-start.2
  3.4 0.7 copy-start.3

commit v4 on v3

--- a/solution.py
+++ b/solution.py
@@ -62,9 +62,7 @@
 def kernel(
     count_ref,
     tiles_ref,
-    row_ref,
-    owner_ref,
-    sub_ref,
+    places_ref,
     times_ref,
     update_ref,
     residual_ref,
@@ -267,7 +265,8 @@
     norm_start(0, norm_part(data))
     lanes = lax.broadcasted_iota(jnp.int32, (128, 128), 1)
 
-    owner = owner_ref[...]
+    places = places_ref[...]
+    owner = places >> 9
     shift = (
         (((owner >> 5) - z) & 3) * 32
         + (((owner >> 3) - x) & 3) * 8
@@ -301,8 +300,8 @@
     to_scalars = pltpu.make_async_copy(order_row, order, order_sem)
     to_scalars.start()
 
-    live_row = jnp.where(lane_row < count_ref[0], row_ref[...], 31)
-    payload = (live_row + 32 * sub_ref[...]).astype(F32)
+    live_row = jnp.where(lane_row < count_ref[0], places & 15, 31)
+    payload = (live_row + 32 * ((places >> 4) & 31)).astype(F32)
     slot = lax.broadcasted_iota(jnp.int32, (8, 256), 0) >> 2
     for g in range(GROUPS):
         for i in range(GROUP):
@@ -413,8 +412,6 @@
         in_specs=[
             pl.BlockSpec(memory_space=pltpu.SMEM),
             pl.BlockSpec(memory_space=pl.ANY),
-            vmem,
-            vmem,
             vmem,
             vmem,
         ],
@@ -452,9 +449,7 @@
     )(
         tile_count,
         tile_values,
-        tile_row.reshape(1, tiles),
-        tile_owner.reshape(1, tiles),
-        tile_sub.reshape(1, tiles),
+        (tile_row + 16 * tile_sub + 512 * tile_owner[:, 0]).reshape(1, tiles),
         residual_times,
     )
     return update, residual[0:4, 0]

time: 74.1 us -> 73.3 us (0.989)
  local copies, waits for them, and re-layouts: 4.04 us -> 2.01 us
  other arithmetic: 0 us -> 1.38 us
    unnamed x9 -> x3, local copies, waits for them, and re-layouts: 3.42 us -> 1.39 us
where the time goes in v4:
time: 73.3 us; the launch traced here: 73.1 us
  Pallas kernels  68.4 us (93%)
  local copies, waits for them, and re-layouts  2.01 us (3%)
  other arithmetic  1.38 us (2%)
  between operations  1.29 us (2%)
    pallas_call x1, Pallas kernels, per_device(): pl.pallas_call(kernel, out_shape=(jax.ShapeDtypeStruct((4, 4096), F32), j...  68.4 us

profile of v4, /device:TPU:1, one launch (start us, length us, event | category | flops | bytes accessed | tf_op | source)
XLA Modules:
  0.0 73.1 jit_solution(925110037239673606)
XLA Ops:
  1.3 0.7 broadcast_multiply_fusion
  2.0 0.7 add_add_fusion
  2.7 0.0 copy-start
  2.7 0.8 %copy-done = f32[4,2048]{1,0:T(4,128)S(1)} copy-done((f32[4,2048]{1,0:T(4,128)S(1)}, f32[4,2048]{1,0:T(4,128)}, u32[]{:S(2)}) %copy-start) | copy-done | bytes 32792
  3.4 68.4 %lsqr.1 = (f32[4,4096]{1,0:T(4,128)S(1)}, f32[8,128]{1,0:T(8,128)S(1)}) custom-call(s32[1]{0:T(128)S(6)} %copy.9.count_ref, f32[256,128,128]{2,1,0:T(8,128)} %tiles_ref.1, s32[1,256]{1,0:T(1,128)S(1)} %bitcast.2, f32[4,2048]{1,0:T(4,128)S(1)} %copy-done), custom_call_target="tpu_custom_call" | custom-call | tf_op jit(solution)/shard_map/lsqr/pallas_call | solution.py:406
  71.8 0.6 slice_reduce_fusion
  72.4 0.6 copy.10
Async XLA Ops:
  2.7 0.8 %copy-start = (f32[4,2048]{1,0:T(4,128)S(1)}, f32[4,2048]{1,0:T(4,128)}, u32[]{:S(2)}) copy-start(f32[4,2048]{1,0:T(4,128)} %times_ref.1) | copy-start | bytes 98308

commit v5 on v4

--- a/solution.py
+++ b/solution.py
@@ -163,7 +163,8 @@
 
     def group_send(turn, g, sign):
         def one(k, device):
-            send_norm(turn, device)
+            if sign > 0:
+                send_norm(turn, device)
             if turn == 0:
                 send_id(k, device)
             pltpu.make_async_remote_copy(
@@ -243,6 +244,7 @@
 
         for g in FORWARD_SENDS:
             group_send(turn, g, -1)
+        all_partners(lambda k, device: send_norm(turn, device))
 
     def forward_finish(turn):
         for g in FORWARD_TURNS:

time: 73.3 us -> 72 us (0.982)
  Pallas kernels: 68.4 us -> 67.1 us
    pallas_call x1, Pallas kernels: 68.4 us -> 67.1 us  [per_device(): pl.pallas_call(kernel, out_shape=(jax.ShapeDtypeStruct((4, 4096), F32), j...]
where the time goes in v5:
time: 72 us; the launch traced here: 71.8 us
  Pallas kernels  67.1 us (93%)
  local copies, waits for them, and re-layouts  2.01 us (3%)
  other arithmetic  1.38 us (2%)
  between operations  1.29 us (2%)
    pallas_call x1, Pallas kernels, per_device(): pl.pallas_call(kernel, out_shape=(jax.ShapeDtypeStruct((4, 4096), F32), j...  67.1 us

profile of v5, /device:TPU:1, one launch (start us, length us, event | category | flops | bytes accessed | tf_op | source)
XLA Modules:
  0.0 71.8 jit_solution(2937288208880082188)
XLA Ops:
  1.3 0.7 broadcast_multiply_fusion
  2.0 0.7 add_add_fusion
  2.7 0.0 copy-start
  2.7 0.8 %copy-done = f32[4,2048]{1,0:T(4,128)S(1)} copy-done((f32[4,2048]{1,0:T(4,128)S(1)}, f32[4,2048]{1,0:T(4,128)}, u32[]{:S(2)}) %copy-start) | copy-done | bytes 32792
  3.4 67.1 %lsqr.1 = (f32[4,4096]{1,0:T(4,128)S(1)}, f32[8,128]{1,0:T(8,128)S(1)}) custom-call(s32[1]{0:T(128)S(6)} %copy.9.count_ref, f32[256,128,128]{2,1,0:T(8,128)} %tiles_ref.1, s32[1,256]{1,0:T(1,128)S(1)} %bitcast.2, f32[4,2048]{1,0:T(4,128)S(1)} %copy-done), custom_call_target="tpu_custom_call" | custom-call | tf_op jit(solution)/shard_map/lsqr/pallas_call | solution.py:408
  70.5 0.6 slice_reduce_fusion
  71.2 0.6 copy.10
Async XLA Ops:
  2.7 0.8 %copy-start = (f32[4,2048]{1,0:T(4,128)S(1)}, f32[4,2048]{1,0:T(4,128)}, u32[]{:S(2)}) copy-start(f32[4,2048]{1,0:T(4,128)} %times_ref.1) | copy-start | bytes 98308
